TPU v7x, 512 devices: a whole 4x4x16 slice. The times are simulated.
512 devices in a mesh: tm: 16 (over x, y_hi, core), height: 16 (over z), mp: 2 (over y_lo).
Axes of the slice: x: 4, y: 4 (y_hi: 2, y_lo: 2; y = y_hi * 2 + y_lo), z: 16, core: 2. Of those that a mesh axis runs over, the one named last changes fastest.
Arguments:
- queries: bfloat16 [16, 16, 384, 1536], P('tm', 'height', None, 'mp'), may hold values from -6 to 6
- key_field: bfloat16 [16, 16, 384, 1536], P('tm', 'height', None, 'mp'), may hold values from -10 to 10
- value_field: bfloat16 [16, 16, 384, 1536], P('tm', 'height', None, 'mp'), may hold values from -6 to 6
- stream: bfloat16 [16, 16, 384, 3072], P('tm', 'height', None, 'mp'), may hold values from -3 to 3
- gate_scale: float32 [3072], P('mp'), may hold values from 0.5 to 1.5
- out_weight: bfloat16 [1536, 3072], P('height', 'mp'), may hold values from -0.15625 to 0.15625
- tile_lists: int32 [16, 16, 9], P('tm', 'height'), may hold values from -1 to 255, as said below
Outputs:
- block_out: bfloat16 [16, 16, 384, 3072], P('tm', 'height', None, 'mp')
Inputs may be any that keep to these rules, and one draw needn't show every extreme that they name: `tile_lists`: entry e names tile (e // 16, e % 16). The list of tile (a, b) names distinct tiles in increasing order, followed by -1 entries; they are all tiles of a box whose first indices form a run within a - 1 to a + 1 inside the same video (same a // 16) and whose second indices form a run within b - 1 to b + 1 inside the same column tile (same b // 16), and the box holds tile (a, b). Some list names 9 tiles and some list holds -1.
All inputs are finite; a program needn't handle non-finite values.
Results may differ from a plain program's by a relative error of at most 0.0059.
Values may be sent and summed in bfloat16 or wider, within the bound.
A program may use at most 128 MiB of HBM per device.

v0:
```python
import math
import jax
import jax.numpy as jnp
from jax import lax
from jax.sharding import PartitionSpec as P

HD = 128


def with_halo(cells, sides, width):
    for axis, dim in sides:
        count = lax.axis_size(axis)
        ends = count - 1
        head = lax.slice_in_dim(cells, 0, width, axis=dim)
        tail = lax.slice_in_dim(cells, cells.shape[dim] - width, cells.shape[dim], axis=dim)
        cells = jnp.concatenate(
            [
                lax.ppermute(tail, axis, [(i, (i + 1) % count) for i in range(ends)]),
                cells,
                lax.ppermute(head, axis, [((i + 1) % count, i) for i in range(ends)]),
            ],
            axis=dim,
        )
    return cells


def slot_mask(tile_lists, frame_index, row_index, frame_count, row_count):
    offsets = jnp.arange(3, dtype=jnp.int32) - 1
    slot_frames = frame_index + offsets[:, None]
    slot_rows = row_index + offsets[None, :]
    slot_ids = slot_frames * row_count + slot_rows
    inside = (
        (slot_frames >= 0)
        & (slot_frames < frame_count)
        & (slot_rows >= 0)
        & (slot_rows < row_count)
    )
    listed = tile_lists.reshape(-1)
    named = jnp.any(slot_ids[:, :, None] == listed[None, None, :], axis=2)
    return named & inside


def dense_heads(query_rows, beside_all, chosen, head_count):
    tokens = query_rows.shape[0]
    key_rows = beside_all[0].reshape(9 * tokens, -1)
    value_rows = beside_all[1].reshape(9 * tokens, -1)
    key_bias = jnp.where(jnp.repeat(chosen.reshape(9), tokens), 0.0, -jnp.inf).astype(jnp.float32)
    score_scale = 1.0 / math.sqrt(HD)
    outputs = []
    for head_index in range(head_count):
        lower = head_index * HD
        upper = lower + HD
        scores = (
            lax.dot_general(
                query_rows[:, lower:upper],
                key_rows[:, lower:upper],
                (((1,), (1,)), ((), ())),
                preferred_element_type=jnp.float32,
            )
            * score_scale
            + key_bias[None, :]
        )
        row_max = jnp.max(scores, axis=1, keepdims=True)
        weights = jnp.exp(scores - row_max).astype(jnp.bfloat16)
        total = jnp.sum(weights.astype(jnp.float32), axis=1, keepdims=True)
        outputs.append(
            jnp.dot(weights, value_rows[:, lower:upper], preferred_element_type=jnp.float32) / total
        )
    return jnp.concatenate(outputs, axis=1).astype(jnp.bfloat16)


def local(queries, key_field, value_field, stream, gate_scale, out_weight, tile_lists):
    groups_here, strips_here, cells_here, channels = queries.shape
    tokens = groups_here * strips_here * cells_here
    head_count = channels // HD
    query_rows = queries.reshape(tokens, channels)
    paired = jnp.stack(
        [key_field.reshape(tokens, channels), value_field.reshape(tokens, channels)]
    ).reshape(2, 1, 1, tokens, channels)
    beside_all = with_halo(paired, (("tm", 1), ("height", 2)), 1)
    frame_index = lax.axis_index("tm")
    row_index = lax.axis_index("height")
    frame_count = lax.axis_size("tm")
    row_count = lax.axis_size("height")
    chosen = slot_mask(tile_lists, frame_index, row_index, frame_count, row_count)
    attended = dense_heads(query_rows, beside_all, chosen, head_count)
    gathered = lax.all_gather(attended, "mp", axis=1, tiled=True)
    full_weight = lax.all_gather(out_weight, "height", axis=0, tiled=True)
    mixed = jnp.dot(gathered, full_weight, preferred_element_type=jnp.float32)
    result = stream.reshape(tokens, -1).astype(jnp.float32) + gate_scale[None, :] * mixed
    return result.astype(jnp.bfloat16).reshape(stream.shape)


def solution(mesh):
    placed = (
        P("tm", "height", None, "mp"),
        P("tm", "height", None, "mp"),
        P("tm", "height", None, "mp"),
        P("tm", "height", None, "mp"),
        P("mp"),
        P("height", "mp"),
        P("tm", "height", None),
    )
    return jax.shard_map(
        local, mesh=mesh, in_specs=placed, out_specs=P("tm", "height", None, "mp"), check_vma=False
    )
```

profile of v0, /device:TPU:10, one launch (start us, length us, event | category | flops | bytes accessed | tf_op | source)
XLA Modules:
  0.0 287.1 jit_solution(8467454233105034597)
XLA Ops:
  6.5 0.0 copy-start.3
  6.5 0.0 all-gather.3.cloned.1.call-start
  6.5 1.4 maximum_bitcast_fusion
  7.9 3.6 %collective-permute-start.1 = (bf16[2,1,1,384,768]{4,3,0,2,1:T(8,128)(2,1)S(1)}, bf16[2,1,1,384,768]{4,3,0,2,1:T(8,128)(2,1)S(1)}, u32[]{:S(2)}, u32[]{:S(2)}) collective-permute-start(bf16[2,1,1,384,768]{4,3,0,2,1:T(8,128)(2,1)S(1)} %maximum_bitcast_fusion), channel_id=1, source_target_pairs={{32,0},{64,32},{96,64},{128,96},{160,128},{192,160},{224,192},{256... | collective-permute-start | bytes 3538952 | tf_op jit(solution)/shard_map/ppermute | solution.py:20
  11.5 1.9 collective-permute-start
  13.5 11.8 %collective-permute-done.1 = bf16[2,1,1,384,768]{4,3,0,2,1:T(8,128)(2,1)S(1)} collective-permute-done((bf16[2,1,1,384,768]{4,3,0,2,1:T(8,128)(2,1)S(1)}, bf16[2,1,1,384,768]{4,3,0,2,1:T(8,128)(2,1)S(1)}, u32[]{:S(2)}, u32[]{:S(2)}) %collective-permute-start.1) | collective-permute-done | bytes 1179680 | tf_op jit(solution)/shard_map/ppermute | solution.py:20
  25.3 6.3 %collective-permute-done = bf16[2,1,1,384,768]{4,3,0,2,1:T(8,128)(2,1)S(1)} collective-permute-done((bf16[2,1,1,384,768]{4,3,0,2,1:T(8,128)(2,1)S(1)}, bf16[2,1,1,384,768]{4,3,0,2,1:T(8,128)(2,1)S(1)}, u32[]{:S(2)}, u32[]{:S(2)}) %collective-permute-start) | collective-permute-done | bytes 1179680 | tf_op jit(solution)/shard_map/ppermute | solution.py:18
  31.6 1.9 pad_maximum_fusion.1
  33.5 1.3 collective-permute-start.3
  34.8 6.3 %collective-permute-start.2 = (bf16[2,3,1,384,768]{4,3,0,2,1:T(8,128)(2,1)}, bf16[2,3,1,384,768]{4,3,0,2,1:T(8,128)(2,1)}, u32[]{:S(2)}, u32[]{:S(2)}) collective-permute-start(bf16[2,3,1,384,768]{4,3,0,2,1:T(8,128)(2,1)} %pad_maximum_fusion.1), channel_id=1, source_target_pairs={{0,2},{2,4},{4,6},{6,8},{8,10},{10,12},{12,14},{14,16},{16,18},{18... | collective-permute-start | bytes 10616840 | tf_op jit(solution)/shard_map/ppermute | solution.py:18
  41.1 0.1 broadcast_add_fusion
  41.2 0.0 copy-done.3
  41.2 0.2 compare_reduce_fusion
  41.4 0.1 and_select_fusion
  41.5 0.1 select_n.16
  41.6 0.7 broadcast_in_dim.12
  42.2 0.7 select_n.17
  43.0 65.0 %collective-permute-done.3 = bf16[2,3,1,384,768]{4,3,0,2,1:T(8,128)(2,1)} collective-permute-done((bf16[2,3,1,384,768]{4,3,0,2,1:T(8,128)(2,1)}, bf16[2,3,1,384,768]{4,3,0,2,1:T(8,128)(2,1)}, u32[]{:S(2)}, u32[]{:S(2)}) %collective-permute-start.3) | collective-permute-done | bytes 3538976 | tf_op jit(solution)/shard_map/ppermute | solution.py:20
  108.0 1.7 collective-permute-done.2
  109.7 8.2 %pad_maximum_fusion = bf16[2,3,3,384,768]{4,3,0,2,1:T(8,128)(2,1)} fusion(bf16[2,3,1,384,768]{4,3,0,2,1:T(8,128)(2,1)} %collective-permute-done.3, bf16[2,1,1,384,768]{4,3,0,2,1:T(8,128)(2,1)S(1)} %collective-permute-done.1, bf16[2,1,1,384,768]{4,3,0,2,1:T(8,128)(2,1)S(1)} %maximum_bitcast_fusion, bf16[2,1,1,384,768]{4,3,0,2,1:T(8,128)(2,1)S(1)} %collective-permute-done, ...), kind=kLoop, calls=%fused_computation | loop fusion | flops 21233664 | bytes 21233664 | tf_op jit(solution)/shard_map/concatenate | solution.py:16
  117.9 0.0 copy-start.2
  117.9 8.9 %fusion.42 = (bf16[1,3,3,384,768]{4,3,0,2,1:T(8,128)(2,1)}, bf16[1,3,3,384,768]{4,3,0,2,1:T(8,128)(2,1)}) fusion(bf16[2,3,3,384,768]{4,3,0,2,1:T(8,128)(2,1)} %pad_maximum_fusion), kind=kLoop, calls=%fused_computation.77 | loop fusion | bytes 21233664 | tf_op jit(solution)/shard_map/slice | solution.py:45
  126.8 0.0 copy-start
  126.8 0.0 copy-done.2
  126.8 3.2 %fusion.43 = (f32[384]{0:T(512)S(1)}, f32[3456,384]{1,0:T(8,128)S(1)}) fusion(f32[3456]{0:T(1024)S(1)} %select_n.17, bf16[384,768]{1,0:T(8,128)(2,1)S(1)} %bitcast.31, bf16[3456,768]{1,0:T(8,128)(2,1)} %bitcast.23), kind=kOutput, calls=%fused_computation.78 | convolution fusion | flops 343719552 | bytes 6309376 | tf_op jit(solution)/shard_map/dot_general | solution.py:54
  130.0 0.0 copy-done
  130.1 1.1 fusion.44
  131.1 1.0 fusion.45
  132.2 1.1 fusion.46
  133.2 0.0 slice-start
  133.2 1.1 fusion.47
  134.3 0.0 slice-start.1
  134.3 1.1 fusion.48
  135.4 0.8 convert_reduce_fusion.5
  136.2 0.0 slice-done
  136.2 0.0 slice-done.1
  136.2 0.9 fusion.10
  137.2 0.8 convert_reduce_fusion.4
  138.0 0.9 fusion.12
  139.0 0.8 convert_reduce_fusion.3
  139.8 1.0 fusion.14
  140.8 0.9 convert_reduce_fusion.2
  141.6 1.0 fusion.16
  142.6 1.1 convert_reduce_fusion.1
  143.7 0.9 fusion.18
  144.6 0.8 convert_reduce_fusion
  145.5 0.0 copy-start.4
  145.5 0.0 copy-start.5
  145.5 0.9 fusion.20
  146.4 0.0 copy-start.1
  146.4 0.8 copy-done.1
  147.2 0.0 all-gather.3.cloned.1.call-update
  147.3 0.0 all-gather.5.cloned.1.call-start
  147.3 0.7 all-gather.5.cloned.1.call-update
  148.0 42.3 %all-gather.3.cloned.1.call-done = bf16[384,1536]{1,0:T(8,128)(2,1)} async-done(((bf16[384,768]{1,0:T(8,128)(2,1)}), bf16[384,1536]{1,0:T(8,128)(2,1)}) %all-gather.3.cloned.1.call-update) | async-done | bytes 1179664 | tf_op jit(solution)/shard_map/all_gather | solution.py:87
  190.4 84.1 %all-gather.5.cloned.1.call-done = bf16[1536,1536]{1,0:T(8,128)(2,1)} async-done(((bf16[96,1536]{1,0:T(8,128)(2,1)}), bf16[1536,1536]{1,0:T(8,128)(2,1)}) %all-gather.5.cloned.1.call-update) | async-done | bytes 4718608 | tf_op jit(solution)/shard_map/all_gather | solution.py:88
  274.5 0.0 copy-done.4
  274.5 0.0 copy-done.5
  274.5 5.7 %fusion.8 = bf16[1,1,384,1536]{3,2,1,0:T(8,128)(2,1)} fusion(bf16[384,1536]{1,0:T(8,128)(2,1)} %all-gather.3.cloned.1.call-done, bf16[1536,1536]{1,0:T(8,128)(2,1)} %all-gather.5.cloned.1.call-done, bf16[1,1,384,1536]{3,2,1,0:T(8,128)(2,1)S(1)} %copy-done.4, f32[1536]{0:T(1024)S(1)} %copy-done.5), kind=kOutput, calls=%fused_computation.29 | convolution fusion | flops 1814298624 | bytes 8263680 | tf_op jit(solution)/shard_map/dot_general | solution.py:89
  (4 shorter events, 0.0 us)
Async XLA Ops:
  6.5 34.6 %copy-start.3 = (s32[1,1,9]{2,1,0:T(1,128)S(1)}, s32[1,1,9]{2,1,0:T(1,128)}, u32[]{:S(2)}) copy-start(s32[1,1,9]{2,1,0:T(1,128)} %param.13) | copy-start | bytes 112
  6.5 183.8 %all-gather.3.cloned.1.call-start = ((), (), s32[]{:S(2)}) async-start(), calls=%async_computation | async-start | bytes 1769472 | tf_op jit(solution)/shard_map/all_gather | solution.py:87
  7.9 17.4 %collective-permute-start.1 = (bf16[2,1,1,384,768]{4,3,0,2,1:T(8,128)(2,1)S(1)}, bf16[2,1,1,384,768]{4,3,0,2,1:T(8,128)(2,1)S(1)}, u32[]{:S(2)}, u32[]{:S(2)}) collective-permute-start(bf16[2,1,1,384,768]{4,3,0,2,1:T(8,128)(2,1)S(1)} %maximum_bitcast_fusion), channel_id=1, source_target_pairs={{32,0},{64,32},{96,64},{128,96},{160,128},{192,160},{224,192},{256... | collective-permute-start | bytes 3538952 | tf_op jit(solution)/shard_map/ppermute | solution.py:20
  11.5 20.0 %collective-permute-start = (bf16[2,1,1,384,768]{4,3,0,2,1:T(8,128)(2,1)S(1)}, bf16[2,1,1,384,768]{4,3,0,2,1:T(8,128)(2,1)S(1)}, u32[]{:S(2)}, u32[]{:S(2)}) collective-permute-start(bf16[2,1,1,384,768]{4,3,0,2,1:T(8,128)(2,1)S(1)} %maximum_bitcast_fusion), channel_id=1, source_target_pairs={{0,32},{32,64},{64,96},{96,128},{128,160},{160,192},{192,224},{224... | collective-permute-start | bytes 3538952 | tf_op jit(solution)/shard_map/ppermute | solution.py:18
  33.5 74.5 %collective-permute-start.3 = (bf16[2,3,1,384,768]{4,3,0,2,1:T(8,128)(2,1)}, bf16[2,3,1,384,768]{4,3,0,2,1:T(8,128)(2,1)}, u32[]{:S(2)}, u32[]{:S(2)}) collective-permute-start(bf16[2,3,1,384,768]{4,3,0,2,1:T(8,128)(2,1)} %pad_maximum_fusion.1), channel_id=1, source_target_pairs={{2,0},{4,2},{6,4},{8,6},{10,8},{12,10},{14,12},{16,14},{18,16},{20... | collective-permute-start | bytes 10616840 | tf_op jit(solution)/shard_map/ppermute | solution.py:20
  34.8 74.9 %collective-permute-start.2 = (bf16[2,3,1,384,768]{4,3,0,2,1:T(8,128)(2,1)}, bf16[2,3,1,384,768]{4,3,0,2,1:T(8,128)(2,1)}, u32[]{:S(2)}, u32[]{:S(2)}) collective-permute-start(bf16[2,3,1,384,768]{4,3,0,2,1:T(8,128)(2,1)} %pad_maximum_fusion.1), channel_id=1, source_target_pairs={{0,2},{2,4},{4,6},{6,8},{8,10},{10,12},{12,14},{14,16},{16,18},{18... | collective-permute-start | bytes 10616840 | tf_op jit(solution)/shard_map/ppermute | solution.py:18
  117.9 8.9 %copy-start.2 = (bf16[1,1,384,768]{3,2,1,0:T(8,128)(2,1)S(1)}, bf16[1,1,384,768]{3,2,1,0:T(8,128)(2,1)}, u32[]{:S(2)}) copy-start(bf16[1,1,384,768]{3,2,1,0:T(8,128)(2,1)} %param.7) | copy-start | bytes 1769476
  126.8 3.3 %copy-start = (bf16[1,3,3,384,768]{4,3,0,2,1:T(8,128)(2,1)S(1)}, bf16[1,3,3,384,768]{4,3,0,2,1:T(8,128)(2,1)}, u32[]{:S(2)}) copy-start(bf16[1,3,3,384,768]{4,3,0,2,1:T(8,128)(2,1)} %get-tuple-element.5) | copy-start | bytes 15925252
  133.2 3.0 %slice-start = ((s8[5308416]{0:T(1024)(128)(4,1)}), s8[4194304]{0:T(1024)(128)(4,1)S(1)}, s32[]{:S(2)}) async-start(s8[5308416]{0:T(1024)(128)(4,1)} %bitcast.15), calls=%async_computation.2 | async-start | bytes 8388608
  134.3 1.9 slice-start.1
  145.5 129.0 %copy-start.4 = (bf16[1,1,384,1536]{3,2,1,0:T(8,128)(2,1)S(1)}, bf16[1,1,384,1536]{3,2,1,0:T(8,128)(2,1)}, u32[]{:S(2)}) copy-start(bf16[1,1,384,1536]{3,2,1,0:T(8,128)(2,1)} %param.10) | copy-start | bytes 3538948
  145.5 129.0 %copy-start.5 = (f32[1536]{0:T(1024)S(1)}, f32[1536]{0:T(1024)}, u32[]{:S(2)}) copy-start(f32[1536]{0:T(1024)} %param.11) | copy-start | bytes 18436
  146.4 0.8 copy-start.1
  147.3 127.2 %all-gather.5.cloned.1.call-start = ((), (), s32[]{:S(2)}) async-start(), calls=%async_computation.1 | async-start | bytes 5013504 | tf_op jit(solution)/shard_map/all_gather | solution.py:88
Sparse Core Ops, SparseCore 0:
  147.4 42.9 all-gather.2
  192.4 82.0 all-gather.4
where the time goes:
time: 287 us
  waiting for transfers between devices  212 us (74%)
  matrix products  20 us (7%)
  other arithmetic  17.2 us (6%)
  between operations  13.5 us (5%)
  starting transfers between devices  13.2 us (5%)
  local copies, waits for them, and re-layouts  11.3 us (4%)
    all_gather x1, waiting for transfers between devices, local(): full_weight = lax.all_gather(out_weight, 'height', axis=0, tiled=True)  84.1 us
    ppermute x2, waiting for transfers between devices, with_halo(): lax.ppermute(head, axis, [((i + 1) % count, i) for i in range(ends)])  76.8 us
    all_gather x1, waiting for transfers between devices, local(): gathered = lax.all_gather(attended, 'mp', axis=1, tiled=True)  42.3 us
    concatenate x2, other arithmetic, with_halo(): jnp.concatenate([lax.ppermute(tail, axis, [(i, (i + 1) % count) for i in...  10.1 us
    slice x1, local copies, waits for them, and re-layouts, dense_heads(): key_rows = beside_all[0].reshape(9 * tokens, -1)  8.92 us
    dot_general x6, matrix products, dense_heads(): lax.dot_general(query_rows[:, lower:upper], key_rows[:, lower:upper], (((...  8.54 us
    ppermute x2, starting transfers between devices, with_halo(): lax.ppermute(tail, axis, [(i, (i + 1) % count) for i in range(ends)])  8.22 us
    ppermute x2, waiting for transfers between devices, with_halo(): lax.ppermute(tail, axis, [(i, (i + 1) % count) for i in range(ends)])  8.02 us
  transfers between devices with their start and end apart: 6, of which 6 were waited for; matrix products, arithmetic and copies ran while one was open for 1% of the time, Pallas kernels for 0%

commit v1 on v0

--- a/solution.py
+++ b/solution.py
@@ -5,6 +5,28 @@
 from jax.sharding import PartitionSpec as P
 
 HD = 128
+
+
+def in_order(parts, dim):
+    shape = list(parts.shape[1:])
+    shape[dim] *= parts.shape[0]
+    return jnp.moveaxis(parts, 0, dim).reshape(shape)
+
+
+def ring_gather(x, axis, dim):
+    length = lax.axis_size(axis)
+    pairs = [(i, (i + 1) % length) for i in range(length)]
+    back = [(b, a) for a, b in pairs]
+    lower, upper = ([], [])
+    for step in range(length - 1):
+        if step % 2 == 0:
+            lower.append(lax.ppermute(lower[-1] if lower else x, axis, pairs))
+        else:
+            upper.append(lax.ppermute(upper[-1] if upper else x, axis, back))
+    blocks = jnp.stack([*lower[::-1], x, *upper])
+    shift = lax.axis_index(axis) - len(lower)
+    blocks = blocks[(jnp.arange(length) - shift) % length]
+    return in_order(blocks, dim)
 
 
 def with_halo(cells, sides, width):
@@ -85,7 +107,7 @@
     chosen = slot_mask(tile_lists, frame_index, row_index, frame_count, row_count)
     attended = dense_heads(query_rows, beside_all, chosen, head_count)
     gathered = lax.all_gather(attended, "mp", axis=1, tiled=True)
-    full_weight = lax.all_gather(out_weight, "height", axis=0, tiled=True)
+    full_weight = ring_gather(out_weight, "height", 0)
     mixed = jnp.dot(gathered, full_weight, preferred_element_type=jnp.float32)
     result = stream.reshape(tokens, -1).astype(jnp.float32) + gate_scale[None, :] * mixed
     return result.astype(jnp.bfloat16).reshape(stream.shape)

time: 287 us -> 265 us (0.923)
  the two profiles are of different devices: /device:TPU:10 before, /device:TPU:1 now
where the time goes in v1:
time: 265 us; the launch traced here: 264 us
  waiting for transfers between devices  112 us (42%)
  starting transfers between devices  64.9 us (24%)
  local copies, waits for them, and re-layouts  39.2 us (15%)
  matrix products  20 us (8%)
  between operations  13.8 us (5%)
  other arithmetic  13.7 us (5%)
    ppermute x2, waiting for transfers between devices, with_halo(): lax.ppermute(head, axis, [((i + 1) % count, i) for i in range(ends)])  54.3 us
    ppermute x7, starting transfers between devices, ring_gather(): upper.append(lax.ppermute(upper[-1] if upper else x, axis, back))  31.9 us
    all_gather x1, waiting for transfers between devices, local(): gathered = lax.all_gather(attended, 'mp', axis=1, tiled=True)  25.6 us
    ppermute x8, waiting for transfers between devices, ring_gather(): lower.append(lax.ppermute(lower[-1] if lower else x, axis, pairs))  21.7 us
    unnamed x47, local copies, waits for them, and re-layouts  21.5 us
    ppermute x8, starting transfers between devices, ring_gather(): lower.append(lax.ppermute(lower[-1] if lower else x, axis, pairs))  17.8 us
    ppermute x7, waiting for transfers between devices, ring_gather(): upper.append(lax.ppermute(upper[-1] if upper else x, axis, back))  9.45 us
    slice x1, local copies, waits for them, and re-layouts, dense_heads(): key_rows = beside_all[0].reshape(9 * tokens, -1)  8.95 us
  transfers between devices with their start and end apart: 20, of which 10 were waited for; matrix products, arithmetic and copies ran while one was open for 25% of the time, Pallas kernels for 0%

profile of v1, /device:TPU:1, one launch (start us, length us, event | category | flops | bytes accessed | tf_op | source)
XLA Modules:
  0.0 263.7 jit_solution(1291239974521514458)
XLA Ops:
  6.5 4.4 %collective-permute-start.4 = (bf16[96,1536]{1,0:T(8,128)(2,1)}, bf16[96,1536]{1,0:T(8,128)(2,1)S(1)}, u32[]{:S(2)}, u32[]{:S(2)}) collective-permute-start(bf16[96,1536]{1,0:T(8,128)(2,1)} %param.12), channel_id=1, source_target_pairs={{0,2},{2,4},{4,6},{6,8},{8,10},{10,12},{12,14},{14,16},{16,18},{18... | collective-permute-start | bytes 884744 | tf_op jit(solution)/shard_map/ppermute | solution.py:23
  10.9 14.5 %collective-permute-done.4 = bf16[96,1536]{1,0:T(8,128)(2,1)S(1)} collective-permute-done((bf16[96,1536]{1,0:T(8,128)(2,1)}, bf16[96,1536]{1,0:T(8,128)(2,1)S(1)}, u32[]{:S(2)}, u32[]{:S(2)}) %collective-permute-start.4) | collective-permute-done | bytes 294944 | tf_op jit(solution)/shard_map/ppermute | solution.py:23
  25.4 1.9 collective-permute-start.5
  27.3 4.6 %collective-permute-start.12 = (bf16[96,1536]{1,0:T(8,128)(2,1)}, bf16[96,1536]{1,0:T(8,128)(2,1)}, u32[]{:S(2)}, u32[]{:S(2)}) collective-permute-start(bf16[96,1536]{1,0:T(8,128)(2,1)} %param.12), channel_id=1, source_target_pairs={{2,0},{4,2},{6,4},{8,6},{10,8},{12,10},{14,12},{16,14},{18,16},{20... | collective-permute-start | bytes 884744 | tf_op jit(solution)/shard_map/ppermute | solution.py:25
  31.9 3.9 %collective-permute-done.5 = bf16[96,1536]{1,0:T(8,128)(2,1)S(1)} collective-permute-done((bf16[96,1536]{1,0:T(8,128)(2,1)S(1)}, bf16[96,1536]{1,0:T(8,128)(2,1)S(1)}, u32[]{:S(2)}, u32[]{:S(2)}) %collective-permute-start.5) | collective-permute-done | bytes 294944 | tf_op jit(solution)/shard_map/ppermute | solution.py:23
  35.8 1.9 collective-permute-start.6
  37.7 4.6 %collective-permute-start.13 = (bf16[96,1536]{1,0:T(8,128)(2,1)}, bf16[96,1536]{1,0:T(8,128)(2,1)}, u32[]{:S(2)}, u32[]{:S(2)}) collective-permute-start(bf16[96,1536]{1,0:T(8,128)(2,1)} %collective-permute-done.12), channel_id=1, source_target_pairs={{2,0},{4,2},{6,4},{8,6},{10,8},{12,10},{14,12},{16,14},{18,16},{20... | collective-permute-start | bytes 884744 | tf_op jit(solution)/shard_map/ppermute | solution.py:25
  42.3 3.0 %collective-permute-done.6 = bf16[96,1536]{1,0:T(8,128)(2,1)} collective-permute-done((bf16[96,1536]{1,0:T(8,128)(2,1)S(1)}, bf16[96,1536]{1,0:T(8,128)(2,1)}, u32[]{:S(2)}, u32[]{:S(2)}) %collective-permute-start.6) | collective-permute-done | bytes 294944 | tf_op jit(solution)/shard_map/ppermute | solution.py:23
  45.3 1.9 collective-permute-start.7
  47.3 1.4 maximum_bitcast_fusion
  48.6 5.0 %collective-permute-start.1 = (bf16[2,1,1,384,768]{4,3,0,2,1:T(8,128)(2,1)S(1)}, bf16[2,1,1,384,768]{4,3,0,2,1:T(8,128)(2,1)S(1)}, u32[]{:S(2)}, u32[]{:S(2)}) collective-permute-start(bf16[2,1,1,384,768]{4,3,0,2,1:T(8,128)(2,1)S(1)} %maximum_bitcast_fusion), channel_id=1, source_target_pairs={{32,0},{64,32},{96,64},{128,96},{160,128},{192,160},{224,192},{256... | collective-permute-start | bytes 3538952 | tf_op jit(solution)/shard_map/ppermute | solution.py:42
  53.6 4.7 %collective-permute-start = (bf16[2,1,1,384,768]{4,3,0,2,1:T(8,128)(2,1)S(1)}, bf16[2,1,1,384,768]{4,3,0,2,1:T(8,128)(2,1)S(1)}, u32[]{:S(2)}, u32[]{:S(2)}) collective-permute-start(bf16[2,1,1,384,768]{4,3,0,2,1:T(8,128)(2,1)S(1)} %maximum_bitcast_fusion), channel_id=1, source_target_pairs={{0,32},{32,64},{64,96},{96,128},{128,160},{160,192},{192,224},{224... | collective-permute-start | bytes 3538952 | tf_op jit(solution)/shard_map/ppermute | solution.py:40
  58.4 4.9 %collective-permute-start.14 = (bf16[96,1536]{1,0:T(8,128)(2,1)}, bf16[96,1536]{1,0:T(8,128)(2,1)S(1)}, u32[]{:S(2)}, u32[]{:S(2)}) collective-permute-start(bf16[96,1536]{1,0:T(8,128)(2,1)} %collective-permute-done.13), channel_id=1, source_target_pairs={{2,0},{4,2},{6,4},{8,6},{10,8},{12,10},{14,12},{16,14},{18,16},{20... | collective-permute-start | bytes 884744 | tf_op jit(solution)/shard_map/ppermute | solution.py:25
  63.2 1.9 collective-permute-start.8
  65.2 3.4 %collective-permute-done.14 = bf16[96,1536]{1,0:T(8,128)(2,1)S(1)} collective-permute-done((bf16[96,1536]{1,0:T(8,128)(2,1)}, bf16[96,1536]{1,0:T(8,128)(2,1)S(1)}, u32[]{:S(2)}, u32[]{:S(2)}) %collective-permute-start.14) | collective-permute-done | bytes 294944 | tf_op jit(solution)/shard_map/ppermute | solution.py:25
  69.3 4.9 %collective-permute-start.15 = (bf16[96,1536]{1,0:T(8,128)(2,1)S(1)}, bf16[96,1536]{1,0:T(8,128)(2,1)}, u32[]{:S(2)}, u32[]{:S(2)}) collective-permute-start(bf16[96,1536]{1,0:T(8,128)(2,1)S(1)} %collective-permute-done.14), channel_id=1, source_target_pairs={{2,0},{4,2},{6,4},{8,6},{10,8},{12,10},{14,12},{16,14},{18,16},{20... | collective-permute-start | bytes 884744 | tf_op jit(solution)/shard_map/ppermute | solution.py:25
  74.2 1.9 collective-permute-start.9
  76.2 0.9 compare_reduce_fusion
  77.1 3.2 %collective-permute-done.15 = bf16[96,1536]{1,0:T(8,128)(2,1)} collective-permute-done((bf16[96,1536]{1,0:T(8,128)(2,1)S(1)}, bf16[96,1536]{1,0:T(8,128)(2,1)}, u32[]{:S(2)}, u32[]{:S(2)}) %collective-permute-start.15) | collective-permute-done | bytes 294944 | tf_op jit(solution)/shard_map/ppermute | solution.py:25
  80.3 5.1 %collective-permute-start.16 = (bf16[96,1536]{1,0:T(8,128)(2,1)}, bf16[96,1536]{1,0:T(8,128)(2,1)}, u32[]{:S(2)}, u32[]{:S(2)}) collective-permute-start(bf16[96,1536]{1,0:T(8,128)(2,1)} %collective-permute-done.15), channel_id=1, source_target_pairs={{2,0},{4,2},{6,4},{8,6},{10,8},{12,10},{14,12},{16,14},{18,16},{20... | collective-permute-start | bytes 884744 | tf_op jit(solution)/shard_map/ppermute | solution.py:25
  85.8 1.9 collective-permute-start.10
  89.3 2.9 %collective-permute-done.16 = bf16[96,1536]{1,0:T(8,128)(2,1)} collective-permute-done((bf16[96,1536]{1,0:T(8,128)(2,1)}, bf16[96,1536]{1,0:T(8,128)(2,1)}, u32[]{:S(2)}, u32[]{:S(2)}) %collective-permute-start.16) | collective-permute-done | bytes 294944 | tf_op jit(solution)/shard_map/ppermute | solution.py:25
  92.1 5.3 %collective-permute-start.17 = (bf16[96,1536]{1,0:T(8,128)(2,1)}, bf16[96,1536]{1,0:T(8,128)(2,1)}, u32[]{:S(2)}, u32[]{:S(2)}) collective-permute-start(bf16[96,1536]{1,0:T(8,128)(2,1)} %collective-permute-done.16), channel_id=1, source_target_pairs={{2,0},{4,2},{6,4},{8,6},{10,8},{12,10},{14,12},{16,14},{18,16},{20... | collective-permute-start | bytes 884744 | tf_op jit(solution)/shard_map/ppermute | solution.py:25
  97.5 1.9 collective-permute-start.11
  100.5 1.3 collective-permute-start.3
  101.8 4.2 %collective-permute-start.2 = (bf16[2,3,1,384,768]{4,3,0,2,1:T(8,128)(2,1)S(1)}, bf16[2,3,1,384,768]{4,3,0,2,1:T(8,128)(2,1)S(1)}, u32[]{:S(2)}, u32[]{:S(2)}) collective-permute-start(bf16[2,3,1,384,768]{4,3,0,2,1:T(8,128)(2,1)S(1)} %pad_maximum_fusion.1), channel_id=1, source_target_pairs={{0,2},{2,4},{4,6},{6,8},{8,10},{10,12},{12,14},{14,16},{16,18},{18... | collective-permute-start | bytes 10616840 | tf_op jit(solution)/shard_map/ppermute | solution.py:40
  106.0 2.6 collective-permute-start.18
  109.3 1.7 bitcast_dynamic-update-slice_fusion.14
  111.0 1.7 bitcast_dynamic-update-slice_fusion.13
  112.8 0.8 bitcast_dynamic-update-slice_fusion.12
  113.5 1.7 bitcast_dynamic-update-slice_fusion.11
  115.2 1.7 bitcast_dynamic-update-slice_fusion.10
  119.1 1.7 bitcast_dynamic-update-slice_fusion.6
  120.9 1.7 bitcast_dynamic-update-slice_fusion.5
  123.3 1.7 bitcast_dynamic-update-slice_fusion.3
  125.0 54.3 %collective-permute-done.3 = bf16[2,3,1,384,768]{4,3,0,2,1:T(8,128)(2,1)S(1)} collective-permute-done((bf16[2,3,1,384,768]{4,3,0,2,1:T(8,128)(2,1)S(1)}, bf16[2,3,1,384,768]{4,3,0,2,1:T(8,128)(2,1)S(1)}, u32[]{:S(2)}, u32[]{:S(2)}) %collective-permute-start.3) | collective-permute-done | bytes 3538976 | tf_op jit(solution)/shard_map/ppermute | solution.py:42
  179.3 1.2 collective-permute-done.2
  180.5 4.9 %pad_maximum_fusion = bf16[2,3,3,384,768]{4,3,0,2,1:T(8,128)(2,1)} fusion(bf16[2,3,1,384,768]{4,3,0,2,1:T(8,128)(2,1)S(1)} %collective-permute-done.3, bf16[2,1,1,384,768]{4,3,0,2,1:T(8,128)(2,1)S(1)} %collective-permute-done.1, bf16[2,1,1,384,768]{4,3,0,2,1:T(8,128)(2,1)S(1)} %maximum_bitcast_fusion, ...), kind=kLoop, calls=%fused_computation.1 | loop fusion | flops 21233664 | bytes 21233664 | tf_op jit(solution)/shard_map/concatenate | solution.py:38
  185.4 8.9 %fusion.44 = (bf16[1,3,3,384,768]{4,3,0,2,1:T(8,128)(2,1)}, bf16[1,3,3,384,768]{4,3,0,2,1:T(8,128)(2,1)}) fusion(bf16[2,3,3,384,768]{4,3,0,2,1:T(8,128)(2,1)} %pad_maximum_fusion), kind=kLoop, calls=%fused_computation.101 | loop fusion | bytes 21233664 | tf_op jit(solution)/shard_map/slice | solution.py:67
  194.4 3.2 %fusion.45 = (f32[384]{0:T(512)S(1)}, f32[3456,384]{1,0:T(8,128)S(1)}) fusion(f32[3456]{0:T(1024)S(1)} %select_n.41, bf16[384,768]{1,0:T(8,128)(2,1)S(1)} %bitcast.67, bf16[3456,768]{1,0:T(8,128)(2,1)} %bitcast.58), kind=kOutput, calls=%fused_computation.102 | convolution fusion | flops 343719552 | bytes 6309376 | tf_op jit(solution)/shard_map/dot_general | solution.py:76
  197.6 1.1 fusion.46
  198.7 1.0 fusion.47
  199.7 1.1 fusion.48
  200.8 1.1 fusion.49
  201.9 1.1 fusion.50
  202.9 0.8 convert_reduce_fusion.5
  203.8 0.9 fusion.10
  204.7 0.8 convert_reduce_fusion.4
  205.6 0.9 fusion.12
  206.5 0.8 convert_reduce_fusion.3
  207.4 1.0 fusion.14
  208.3 0.9 convert_reduce_fusion.2
  209.2 1.0 fusion.16
  210.2 1.1 convert_reduce_fusion.1
  211.2 0.9 fusion.18
  212.2 0.8 convert_reduce_fusion
  213.0 1.0 fusion.20
  214.0 0.8 copy-done.1
  214.8 1.7 bitcast_dynamic-update-slice_fusion.2
  216.5 1.8 bitcast_dynamic-update-slice_fusion.1
  218.3 1.7 bitcast_dynamic-update-slice_fusion
  220.1 5.4 %gather_fusion = bf16[16,96,1536]{2,1,0:T(8,128)(2,1)} fusion(bf16[16,96,1536]{2,1,0:T(8,128)(2,1)} %bitcast_dynamic-update-slice_fusion, s32[1024]{0:T(1024)} %pad_clamp_fusion), kind=kCustom, calls=%fused_computation | custom fusion | bytes 9437248 | tf_op jit(solution)/shard_map/gather | solution.py:28
  225.5 25.6 %all-gather.2.cloned.1.call-done = bf16[384,1536]{1,0:T(8,128)(2,1)} async-done(((bf16[384,768]{1,0:T(8,128)(2,1)}), bf16[384,1536]{1,0:T(8,128)(2,1)}) %all-gather.2.cloned.1.call-update) | async-done | bytes 1179664 | tf_op jit(solution)/shard_map/all_gather | solution.py:109
  251.1 5.7 %fusion.8 = bf16[1,1,384,1536]{3,2,1,0:T(8,128)(2,1)} fusion(bf16[384,1536]{1,0:T(8,128)(2,1)} %all-gather.2.cloned.1.call-done, bf16[1536,1536]{1,0:T(8,128)(2,1)} %bitcast.64, bf16[1,1,384,1536]{3,2,1,0:T(8,128)(2,1)S(1)} %copy-done.12, f32[1536]{0:T(1024)S(1)} %copy-done.13), kind=kOutput, calls=%fused_computation.30 | convolution fusion | flops 1814298624 | bytes 8263680 | tf_op jit(solution)/shard_map/dot_general | solution.py:111
  (61 shorter events, 7.6 us)
Async XLA Ops:
  6.5 244.6 %all-gather.2.cloned.1.call-start = ((), (), s32[]{:S(2)}) async-start(), calls=%async_computation | async-start | bytes 1769472 | tf_op jit(solution)/shard_map/all_gather | solution.py:109
  6.5 18.9 %collective-permute-start.4 = (bf16[96,1536]{1,0:T(8,128)(2,1)}, bf16[96,1536]{1,0:T(8,128)(2,1)S(1)}, u32[]{:S(2)}, u32[]{:S(2)}) collective-permute-start(bf16[96,1536]{1,0:T(8,128)(2,1)} %param.12), channel_id=1, source_target_pairs={{0,2},{2,4},{4,6},{6,8},{8,10},{10,12},{12,14},{14,16},{16,18},{18... | collective-permute-start | bytes 884744 | tf_op jit(solution)/shard_map/ppermute | solution.py:23
  25.4 21.8 %copy-start.4 = (bf16[96,1536]{1,0:T(8,128)(2,1)}, bf16[96,1536]{1,0:T(8,128)(2,1)S(1)}, u32[]{:S(2)}) copy-start(bf16[96,1536]{1,0:T(8,128)(2,1)S(1)} %collective-permute-done.4) | copy-start | bytes 884740
  25.4 10.4 %collective-permute-start.5 = (bf16[96,1536]{1,0:T(8,128)(2,1)S(1)}, bf16[96,1536]{1,0:T(8,128)(2,1)S(1)}, u32[]{:S(2)}, u32[]{:S(2)}) collective-permute-start(bf16[96,1536]{1,0:T(8,128)(2,1)S(1)} %collective-permute-done.4), channel_id=1, source_target_pairs={{0,2},{2,4},{4,6},{6,8},{8,10},{10,12},{12,14},{14,16},{16,18},{18... | collective-permute-start | bytes 884744 | tf_op jit(solution)/shard_map/ppermute | solution.py:23
  27.3 10.4 %collective-permute-start.12 = (bf16[96,1536]{1,0:T(8,128)(2,1)}, bf16[96,1536]{1,0:T(8,128)(2,1)}, u32[]{:S(2)}, u32[]{:S(2)}) collective-permute-start(bf16[96,1536]{1,0:T(8,128)(2,1)} %param.12), channel_id=1, source_target_pairs={{2,0},{4,2},{6,4},{8,6},{10,8},{12,10},{14,12},{16,14},{18,16},{20... | collective-permute-start | bytes 884744 | tf_op jit(solution)/shard_map/ppermute | solution.py:25
  35.8 11.5 %copy-start.6 = (bf16[96,1536]{1,0:T(8,128)(2,1)}, bf16[96,1536]{1,0:T(8,128)(2,1)S(1)}, u32[]{:S(2)}) copy-start(bf16[96,1536]{1,0:T(8,128)(2,1)S(1)} %collective-permute-done.5) | copy-start | bytes 884740
  35.8 9.6 %collective-permute-start.6 = (bf16[96,1536]{1,0:T(8,128)(2,1)S(1)}, bf16[96,1536]{1,0:T(8,128)(2,1)}, u32[]{:S(2)}, u32[]{:S(2)}) collective-permute-start(bf16[96,1536]{1,0:T(8,128)(2,1)S(1)} %collective-permute-done.5), channel_id=1, source_target_pairs={{0,2},{2,4},{4,6},{6,8},{8,10},{10,12},{12,14},{14,16},{16,18},{18... | collective-permute-start | bytes 884744 | tf_op jit(solution)/shard_map/ppermute | solution.py:23
  37.7 20.6 %collective-permute-start.13 = (bf16[96,1536]{1,0:T(8,128)(2,1)}, bf16[96,1536]{1,0:T(8,128)(2,1)}, u32[]{:S(2)}, u32[]{:S(2)}) collective-permute-start(bf16[96,1536]{1,0:T(8,128)(2,1)} %collective-permute-done.12), channel_id=1, source_target_pairs={{2,0},{4,2},{6,4},{8,6},{10,8},{12,10},{14,12},{16,14},{18,16},{20... | collective-permute-start | bytes 884744 | tf_op jit(solution)/shard_map/ppermute | solution.py:25
  45.3 17.9 %collective-permute-start.7 = (bf16[96,1536]{1,0:T(8,128)(2,1)}, bf16[96,1536]{1,0:T(8,128)(2,1)}, u32[]{:S(2)}, u32[]{:S(2)}) collective-permute-start(bf16[96,1536]{1,0:T(8,128)(2,1)} %collective-permute-done.6), channel_id=1, source_target_pairs={{0,2},{2,4},{4,6},{6,8},{8,10},{10,12},{12,14},{14,16},{16,18},{18... | collective-permute-start | bytes 884744 | tf_op jit(solution)/shard_map/ppermute | solution.py:23
  48.6 51.4 %collective-permute-start.1 = (bf16[2,1,1,384,768]{4,3,0,2,1:T(8,128)(2,1)S(1)}, bf16[2,1,1,384,768]{4,3,0,2,1:T(8,128)(2,1)S(1)}, u32[]{:S(2)}, u32[]{:S(2)}) collective-permute-start(bf16[2,1,1,384,768]{4,3,0,2,1:T(8,128)(2,1)S(1)} %maximum_bitcast_fusion), channel_id=1, source_target_pairs={{32,0},{64,32},{96,64},{128,96},{160,128},{192,160},{224,192},{256... | collective-permute-start | bytes 3538952 | tf_op jit(solution)/shard_map/ppermute | solution.py:42
  53.6 46.4 %collective-permute-start = (bf16[2,1,1,384,768]{4,3,0,2,1:T(8,128)(2,1)S(1)}, bf16[2,1,1,384,768]{4,3,0,2,1:T(8,128)(2,1)S(1)}, u32[]{:S(2)}, u32[]{:S(2)}) collective-permute-start(bf16[2,1,1,384,768]{4,3,0,2,1:T(8,128)(2,1)S(1)} %maximum_bitcast_fusion), channel_id=1, source_target_pairs={{0,32},{32,64},{64,96},{96,128},{128,160},{160,192},{192,224},{224... | collective-permute-start | bytes 3538952 | tf_op jit(solution)/shard_map/ppermute | solution.py:40
  58.4 10.2 %collective-permute-start.14 = (bf16[96,1536]{1,0:T(8,128)(2,1)}, bf16[96,1536]{1,0:T(8,128)(2,1)S(1)}, u32[]{:S(2)}, u32[]{:S(2)}) collective-permute-start(bf16[96,1536]{1,0:T(8,128)(2,1)} %collective-permute-done.13), channel_id=1, source_target_pairs={{2,0},{4,2},{6,4},{8,6},{10,8},{12,10},{14,12},{16,14},{18,16},{20... | collective-permute-start | bytes 884744 | tf_op jit(solution)/shard_map/ppermute | solution.py:25
  63.2 11.0 %collective-permute-start.8 = (bf16[96,1536]{1,0:T(8,128)(2,1)}, bf16[96,1536]{1,0:T(8,128)(2,1)S(1)}, u32[]{:S(2)}, u32[]{:S(2)}) collective-permute-start(bf16[96,1536]{1,0:T(8,128)(2,1)} %collective-permute-done.7), channel_id=1, source_target_pairs={{0,2},{2,4},{4,6},{6,8},{8,10},{10,12},{12,14},{14,16},{16,18},{18... | collective-permute-start | bytes 884744 | tf_op jit(solution)/shard_map/ppermute | solution.py:23
  68.6 0.7 copy-start.8
  69.3 11.0 %collective-permute-start.15 = (bf16[96,1536]{1,0:T(8,128)(2,1)S(1)}, bf16[96,1536]{1,0:T(8,128)(2,1)}, u32[]{:S(2)}, u32[]{:S(2)}) collective-permute-start(bf16[96,1536]{1,0:T(8,128)(2,1)S(1)} %collective-permute-done.14), channel_id=1, source_target_pairs={{2,0},{4,2},{6,4},{8,6},{10,8},{12,10},{14,12},{16,14},{18,16},{20... | collective-permute-start | bytes 884744 | tf_op jit(solution)/shard_map/ppermute | solution.py:25
  74.2 6.1 %copy-start.10 = (bf16[96,1536]{1,0:T(8,128)(2,1)}, bf16[96,1536]{1,0:T(8,128)(2,1)S(1)}, u32[]{:S(2)}) copy-start(bf16[96,1536]{1,0:T(8,128)(2,1)S(1)} %collective-permute-done.8) | copy-start | bytes 884740
  74.2 11.5 %collective-permute-start.9 = (bf16[96,1536]{1,0:T(8,128)(2,1)S(1)}, bf16[96,1536]{1,0:T(8,128)(2,1)}, u32[]{:S(2)}, u32[]{:S(2)}) collective-permute-start(bf16[96,1536]{1,0:T(8,128)(2,1)S(1)} %collective-permute-done.8), channel_id=1, source_target_pairs={{0,2},{2,4},{4,6},{6,8},{8,10},{10,12},{12,14},{14,16},{16,18},{18... | collective-permute-start | bytes 884744 | tf_op jit(solution)/shard_map/ppermute | solution.py:23
  80.3 11.8 %collective-permute-start.16 = (bf16[96,1536]{1,0:T(8,128)(2,1)}, bf16[96,1536]{1,0:T(8,128)(2,1)}, u32[]{:S(2)}, u32[]{:S(2)}) collective-permute-start(bf16[96,1536]{1,0:T(8,128)(2,1)} %collective-permute-done.15), channel_id=1, source_target_pairs={{2,0},{4,2},{6,4},{8,6},{10,8},{12,10},{14,12},{16,14},{18,16},{20... | collective-permute-start | bytes 884744 | tf_op jit(solution)/shard_map/ppermute | solution.py:25
  85.8 11.7 %collective-permute-start.10 = (bf16[96,1536]{1,0:T(8,128)(2,1)}, bf16[96,1536]{1,0:T(8,128)(2,1)}, u32[]{:S(2)}, u32[]{:S(2)}) collective-permute-start(bf16[96,1536]{1,0:T(8,128)(2,1)} %collective-permute-done.9), channel_id=1, source_target_pairs={{0,2},{2,4},{4,6},{6,8},{8,10},{10,12},{12,14},{14,16},{16,18},{18... | collective-permute-start | bytes 884744 | tf_op jit(solution)/shard_map/ppermute | solution.py:23
  89.3 23.5 %copy-start.11 = (bf16[96,1536]{1,0:T(8,128)(2,1)S(1)}, bf16[96,1536]{1,0:T(8,128)(2,1)}, u32[]{:S(2)}) copy-start(bf16[96,1536]{1,0:T(8,128)(2,1)} %copy-done.10) | copy-start | bytes 884740
  92.1 13.9 %collective-permute-start.17 = (bf16[96,1536]{1,0:T(8,128)(2,1)}, bf16[96,1536]{1,0:T(8,128)(2,1)}, u32[]{:S(2)}, u32[]{:S(2)}) collective-permute-start(bf16[96,1536]{1,0:T(8,128)(2,1)} %collective-permute-done.16), channel_id=1, source_target_pairs={{2,0},{4,2},{6,4},{8,6},{10,8},{12,10},{14,12},{16,14},{18,16},{20... | collective-permute-start | bytes 884744 | tf_op jit(solution)/shard_map/ppermute | solution.py:25
  97.5 11.1 %collective-permute-start.11 = (bf16[96,1536]{1,0:T(8,128)(2,1)}, bf16[96,1536]{1,0:T(8,128)(2,1)S(1)}, u32[]{:S(2)}, u32[]{:S(2)}) collective-permute-start(bf16[96,1536]{1,0:T(8,128)(2,1)} %collective-permute-done.10), channel_id=1, source_target_pairs={{0,2},{2,4},{4,6},{6,8},{8,10},{10,12},{12,14},{14,16},{16,18},{18... | collective-permute-start | bytes 884744 | tf_op jit(solution)/shard_map/ppermute | solution.py:23
  100.0 16.9 %copy-start.7 = (bf16[96,1536]{1,0:T(8,128)(2,1)S(1)}, bf16[96,1536]{1,0:T(8,128)(2,1)}, u32[]{:S(2)}) copy-start(bf16[96,1536]{1,0:T(8,128)(2,1)} %copy-done.6) | copy-start | bytes 884740
  100.0 17.6 %copy-start.5 = (bf16[96,1536]{1,0:T(8,128)(2,1)S(1)}, bf16[96,1536]{1,0:T(8,128)(2,1)}, u32[]{:S(2)}) copy-start(bf16[96,1536]{1,0:T(8,128)(2,1)} %copy-done.4) | copy-start | bytes 884740
  100.0 18.4 %copy-start.3 = (bf16[96,1536]{1,0:T(8,128)(2,1)S(1)}, bf16[96,1536]{1,0:T(8,128)(2,1)}, u32[]{:S(2)}) copy-start(bf16[96,1536]{1,0:T(8,128)(2,1)} %param.12) | copy-start | bytes 884740
  100.0 22.5 %copy-start.9 = (bf16[96,1536]{1,0:T(8,128)(2,1)S(1)}, bf16[96,1536]{1,0:T(8,128)(2,1)}, u32[]{:S(2)}) copy-start(bf16[96,1536]{1,0:T(8,128)(2,1)} %copy-done.8) | copy-start | bytes 884740
  100.5 78.8 %collective-permute-start.3 = (bf16[2,3,1,384,768]{4,3,0,2,1:T(8,128)(2,1)S(1)}, bf16[2,3,1,384,768]{4,3,0,2,1:T(8,128)(2,1)S(1)}, u32[]{:S(2)}, u32[]{:S(2)}) collective-permute-start(bf16[2,3,1,384,768]{4,3,0,2,1:T(8,128)(2,1)S(1)} %pad_maximum_fusion.1), channel_id=1, source_target_pairs={{2,0},{4,2},{6,4},{8,6},{10,8},{12,10},{14,12},{16,14},{18,16},{20... | collective-permute-start | bytes 10616840 | tf_op jit(solution)/shard_map/ppermute | solution.py:42
  101.8 78.7 %collective-permute-start.2 = (bf16[2,3,1,384,768]{4,3,0,2,1:T(8,128)(2,1)S(1)}, bf16[2,3,1,384,768]{4,3,0,2,1:T(8,128)(2,1)S(1)}, u32[]{:S(2)}, u32[]{:S(2)}) collective-permute-start(bf16[2,3,1,384,768]{4,3,0,2,1:T(8,128)(2,1)S(1)} %pad_maximum_fusion.1), channel_id=1, source_target_pairs={{0,2},{2,4},{4,6},{6,8},{8,10},{10,12},{12,14},{14,16},{16,18},{18... | collective-permute-start | bytes 10616840 | tf_op jit(solution)/shard_map/ppermute | solution.py:40
  106.0 112.3 %collective-permute-start.18 = (bf16[96,1536]{1,0:T(8,128)(2,1)}, bf16[96,1536]{1,0:T(8,128)(2,1)}, u32[]{:S(2)}, u32[]{:S(2)}) collective-permute-start(bf16[96,1536]{1,0:T(8,128)(2,1)} %collective-permute-done.17), channel_id=1, source_target_pairs={{2,0},{4,2},{6,4},{8,6},{10,8},{12,10},{14,12},{16,14},{18,16},{20... | collective-permute-start | bytes 884744 | tf_op jit(solution)/shard_map/ppermute | solution.py:25
  185.4 9.0 %copy-start.2 = (bf16[1,1,384,768]{3,2,1,0:T(8,128)(2,1)S(1)}, bf16[1,1,384,768]{3,2,1,0:T(8,128)(2,1)}, u32[]{:S(2)}) copy-start(bf16[1,1,384,768]{3,2,1,0:T(8,128)(2,1)} %param.7) | copy-start | bytes 1769476
  194.3 3.3 %copy-start = (bf16[1,3,3,384,768]{4,3,0,2,1:T(8,128)(2,1)S(1)}, bf16[1,3,3,384,768]{4,3,0,2,1:T(8,128)(2,1)}, u32[]{:S(2)}) copy-start(bf16[1,3,3,384,768]{4,3,0,2,1:T(8,128)(2,1)} %get-tuple-element.5) | copy-start | bytes 15925252
  200.8 3.0 %slice-start = ((s8[5308416]{0:T(1024)(128)(4,1)}), s8[4194304]{0:T(1024)(128)(4,1)S(1)}, s32[]{:S(2)}) async-start(s8[5308416]{0:T(1024)(128)(4,1)} %bitcast.50), calls=%async_computation.1 | async-start | bytes 8388608
  201.9 1.9 slice-start.1
  214.0 0.8 copy-start.1
  216.5 34.6 %copy-start.12 = (bf16[1,1,384,1536]{3,2,1,0:T(8,128)(2,1)S(1)}, bf16[1,1,384,1536]{3,2,1,0:T(8,128)(2,1)}, u32[]{:S(2)}) copy-start(bf16[1,1,384,1536]{3,2,1,0:T(8,128)(2,1)} %param.10) | copy-start | bytes 3538948
  216.5 34.6 %copy-start.13 = (f32[1536]{0:T(1024)S(1)}, f32[1536]{0:T(1024)}, u32[]{:S(2)}) copy-start(f32[1536]{0:T(1024)} %param.11) | copy-start | bytes 18436
Sparse Core Ops, SparseCore 0:
  214.9 36.1 all-gather.1
